TPU v7x, 256 devices: a whole 4x4x8 slice. The times are simulated.
256 devices in a mesh: seq: 32 (over y, x, core), head: 8 (over z).
Axes of the slice: x: 4, y: 4, z: 8, core: 2. Of those that a mesh axis runs over, the one named last changes fastest.
Arguments:
- queries: bfloat16 [65536, 8192], P(('seq', 'head')), may hold values from -8 to 8
- keys: bfloat16 [65536, 1024], P(('seq', 'head')), may hold values from -8 to 8
- values: bfloat16 [65536, 1024], P(('seq', 'head')), may hold values from -6 to 6
- doc_block: int32 [512], replicated, may hold values from 0 to 511, as said below
- balance: int32 [512], replicated, may hold values from 0 to 511, as said below
Outputs:
- attended: bfloat16 [65536, 8192], P(('seq', 'head'))
Inputs may be any that keep to these rules, and one draw needn't show every extreme that they name: `balance`: each value once. Seq group g takes positions g * 16 to (g + 1) * 16 - 1; no two blocks that start in the same seq group (same b // 16) are placed in the same seq group, and every seq group receives blocks from 16 different source groups. `doc_block`: the blocks of one document take consecutive positions of balance inside one seq group, at most 4 of them; in every seq group one document has 4. A document's label is the largest index among its blocks.
All inputs are finite; a program needn't handle non-finite values.
Results may differ from a plain program's by a relative error of at most 0.0046.
Values may be sent and summed in bfloat16 or wider, within the bound.
A program may use at most 128 MiB of HBM per device.

v0:
```python
import math

import jax
import jax.numpy as jnp
from jax import lax
from jax.sharding import PartitionSpec as P

HEAD_DIM = 128
BLOCK = 128
MOSTB = 4


def routes(balance, per_group, seq_count):
    seq_index = lax.axis_index("seq")
    block_total = balance.shape[0]
    capacity = (per_group + seq_count - 1) // seq_count
    positions = jnp.arange(block_total, dtype=jnp.int32)
    within = jnp.arange(per_group, dtype=jnp.int32)
    owned_ids = seq_index * per_group + within
    matches = balance[None, :] == owned_ids[:, None]
    dest_pos = jnp.sum(jnp.where(matches, positions[None, :], 0), axis=1)
    dest_dev = dest_pos // per_group
    before = within[None, :] < within[:, None]
    rank_out = jnp.sum(
        ((dest_dev[None, :] == dest_dev[:, None]) & before).astype(jnp.int32), axis=1
    )
    slot_out = dest_dev * capacity + rank_out
    held_blocks = lax.dynamic_slice_in_dim(balance, seq_index * per_group, per_group)
    src_dev = held_blocks // per_group
    src_slot = held_blocks % per_group
    earlier = (src_dev[None, :] == src_dev[:, None]) & (src_slot[None, :] < src_slot[:, None])
    rank_in = jnp.sum(earlier.astype(jnp.int32), axis=1)
    slot_in = src_dev * capacity + rank_in
    return (dest_pos, slot_out, slot_in, seq_count * capacity)


def fill_slots(blocks, slot_of, slot_count):
    targets = jnp.arange(slot_count, dtype=jnp.int32)
    matches = targets[:, None] == slot_of[None, :]
    source = jnp.sum(
        jnp.where(matches, jnp.arange(slot_of.shape[0], dtype=jnp.int32)[None, :], 0), axis=1
    )
    filled = jnp.any(matches, axis=1)
    picked = jnp.take(blocks, source, axis=0)
    mask_shape = (slot_count,) + (1,) * (blocks.ndim - 1)
    return jnp.where(filled.reshape(mask_shape), picked, jnp.zeros_like(picked))


def window_info(centre_pos, per_group, width, doc_block, balance):
    row_count = centre_pos.shape[0]
    group_start = centre_pos // per_group * per_group
    first_pos = group_start + jnp.clip(centre_pos % per_group - width + 1, 0, per_group - width)
    win_pos = first_pos[:, None] + jnp.arange(width, dtype=jnp.int32)[None, :]
    offsets = jnp.arange(BLOCK, dtype=jnp.int32)
    key_rank = (win_pos[:, :, None] * BLOCK + offsets[None, None, :]).reshape(
        row_count, width * BLOCK
    )
    win_docs = doc_block[balance[win_pos]]
    key_doc = jnp.broadcast_to(win_docs[:, :, None], (row_count, width, BLOCK)).reshape(
        row_count, width * BLOCK
    )
    query_rank = centre_pos[:, None] * BLOCK + offsets[None, :]
    query_doc = doc_block[balance[centre_pos]]
    return (win_pos, (query_rank, query_doc, key_rank, key_doc))


def attend(query_blocks, key_win, value_win, masks, kv_local):
    query_rank, query_doc, key_rank, key_doc = masks
    scale_factor = 1.0 / math.sqrt(HEAD_DIM)

    def one_block(items):
        query_blk, key_part, value_part, row_rank, row_doc, col_rank, col_doc = items
        grouped = query_blk.reshape(BLOCK, kv_local, -1, HEAD_DIM)
        keyed = key_part.reshape(-1, kv_local, HEAD_DIM)
        valued = value_part.reshape(-1, kv_local, HEAD_DIM)
        scores = (
            jnp.einsum("tkgd,ukd->kgtu", grouped, keyed, preferred_element_type=jnp.float32)
            * scale_factor
        )
        allowed = (col_doc[None, :] == row_doc) & (col_rank[None, :] <= row_rank[:, None])
        scores = jnp.where(allowed[None, None, :, :], scores, -jnp.inf)
        top_score = jnp.max(scores, axis=-1, keepdims=True)
        raised = jnp.exp(scores - top_score)
        weights = (raised / jnp.sum(raised, axis=-1, keepdims=True)).astype(jnp.bfloat16)
        mixed = jnp.einsum("kgtu,ukd->tkgd", weights, valued, preferred_element_type=jnp.float32)
        return mixed.reshape(BLOCK, -1).astype(jnp.bfloat16)

    return lax.map(
        one_block, (query_blocks, key_win, value_win, query_rank, query_doc, key_rank, key_doc)
    )


def shards(queries, keys, values, doc_block, balance):
    seq_count = lax.axis_size("seq")
    head_count = lax.axis_size("head")
    tok_dev = queries.shape[0]
    per_group = tok_dev * head_count // BLOCK
    width = min(MOSTB, per_group)
    query_cols = queries.shape[1] // head_count
    kv_cols = keys.shape[1] // head_count
    kv_local = kv_cols // HEAD_DIM
    query_grp, key_grp, value_grp = (
        lax.all_to_all(
            queries.reshape(1, tok_dev, queries.shape[1]),
            "head",
            split_axis=2,
            concat_axis=0,
            tiled=True,
        ),
        lax.all_to_all(
            keys.reshape(1, tok_dev, keys.shape[1]), "head", split_axis=2, concat_axis=0, tiled=True
        ),
        lax.all_to_all(
            values.reshape(1, tok_dev, values.shape[1]),
            "head",
            split_axis=2,
            concat_axis=0,
            tiled=True,
        ),
    )
    query_grp = query_grp.reshape(per_group, BLOCK, query_cols)
    key_grp = key_grp.reshape(per_group, BLOCK, kv_cols)
    value_grp = value_grp.reshape(per_group, BLOCK, kv_cols)
    dest_pos, slot_out, slot_in, slot_count = routes(balance, per_group, seq_count)
    group_base = lax.axis_index("seq") * per_group
    held_pos = group_base + jnp.arange(per_group, dtype=jnp.int32)
    query_arr, key_arr, value_arr = (
        lax.all_to_all(
            fill_slots(query_grp, slot_out, slot_count),
            "seq",
            split_axis=0,
            concat_axis=0,
            tiled=True,
        ),
        lax.all_to_all(
            fill_slots(key_grp, slot_out, slot_count),
            "seq",
            split_axis=0,
            concat_axis=0,
            tiled=True,
        ),
        lax.all_to_all(
            fill_slots(value_grp, slot_out, slot_count),
            "seq",
            split_axis=0,
            concat_axis=0,
            tiled=True,
        ),
    )
    query_bal = jnp.take(query_arr, slot_in, axis=0)
    key_bal = jnp.take(key_arr, slot_in, axis=0)
    value_bal = jnp.take(value_arr, slot_in, axis=0)
    win_pos, masks = window_info(held_pos, per_group, width, doc_block, balance)
    local_win = win_pos - group_base
    key_win = jnp.take(key_bal, local_win, axis=0)
    value_win = jnp.take(value_bal, local_win, axis=0)
    mixed = attend(query_bal, key_win, value_win, masks, kv_local)
    returned = lax.all_to_all(
        fill_slots(mixed, slot_in, slot_count), "seq", split_axis=0, concat_axis=0, tiled=True
    )
    result = jnp.take(returned, slot_out, axis=0)
    finished = lax.all_to_all(
        result.reshape(head_count, tok_dev, query_cols),
        "head",
        split_axis=0,
        concat_axis=2,
        tiled=True,
    )
    return finished.reshape(tok_dev, head_count * query_cols)


def solution(mesh):
    in_specs = (
        P(("seq", "head"), None),
        P(("seq", "head"), None),
        P(("seq", "head"), None),
        P(),
        P(),
    )
    out_specs = P(("seq", "head"), None)
    return jax.shard_map(shards, mesh=mesh, in_specs=in_specs, out_specs=out_specs, check_vma=False)
```

profile of v0, /device:TPU:96, one launch (start us, length us, event | category | flops | bytes accessed | tf_op | source)
XLA Modules:
  0.0 720.9 jit_solution(8045283794661194156)
XLA Ops:
  0.0 2.5 copy.53
  3.0 3.9 reduce.5
  7.9 7.7 %all-to-all-start = ((bf16[8,2,16384]{2,1,0:T(2,128)(2,1)}), bf16[8,2,16384]{2,1,0:T(2,128)(2,1)S(1)}, u32[]{:S(2)}, u32[]{:S(2)}) async-start(bf16[8,2,16384]{2,1,0:T(2,128)(2,1)} %reshape.511), calls=%async_computation | async-start | bytes 1048576 | tf_op jit(solution)/shard_map/all_to_all | solution.py:113
  16.4 3.9 reduce.4
  21.3 7.8 %all-to-all-done = bf16[8,2,16384]{2,1,0:T(2,128)(2,1)S(1)} async-done(((bf16[8,2,16384]{2,1,0:T(2,128)(2,1)}), bf16[8,2,16384]{2,1,0:T(2,128)(2,1)S(1)}, u32[]{:S(2)}, u32[]{:S(2)}) %all-to-all-start) | async-done | bytes 524320 | tf_op jit(solution)/shard_map/all_to_all | solution.py:113
  29.1 7.4 %all-to-all-start.2 = ((bf16[8,2,16384]{2,1,0:T(2,128)(2,1)}), bf16[8,2,16384]{2,1,0:T(2,128)(2,1)S(1)}, u32[]{:S(2)}, u32[]{:S(2)}) async-start(bf16[8,2,16384]{2,1,0:T(2,128)(2,1)} %reshape.513), calls=%async_computation.2 | async-start | bytes 1048576 | tf_op jit(solution)/shard_map/all_to_all | solution.py:110
  36.4 17.8 %copy.57 = bf16[1,256,8192]{1,0,2:T(2,128)(2,1)} copy(bf16[1,256,8192]{2,1,0:T(8,128)(2,1)} %bitcast.107) | data formatting | bytes 8388608 | tf_op jit(solution)/shard_map/reshape | solution.py:104
  54.3 43.5 %reduce.6 = bf16[8192,256]{1,0:T(8,128)(2,1)} reduce(bf16[8192,1,256]{2,1,0:T(2,128)(2,1)} %bitcast.94, bf16[]{:T(256)} %broadcast.519), dimensions={1}, to_apply=%bitcast.65.reduce_sub_computation | reduce | bytes 8388610
  97.8 7.0 reshape.515
  104.8 7.3 %all-to-all-start.4 = ((bf16[8,2,131072]{2,1,0:T(2,128)(2,1)}), bf16[8,2,131072]{2,1,0:T(2,128)(2,1)}, u32[]{:S(2)}, u32[]{:S(2)}) async-start(bf16[8,2,131072]{2,1,0:T(2,128)(2,1)} %reshape.515), calls=%async_computation.4 | async-start | bytes 8388608 | tf_op jit(solution)/shard_map/all_to_all | solution.py:103
  116.2 1.7 select_select_fusion.2
  117.9 82.6 %all-to-all-done.4 = bf16[8,2,131072]{2,1,0:T(2,128)(2,1)} async-done(((bf16[8,2,131072]{2,1,0:T(2,128)(2,1)}), bf16[8,2,131072]{2,1,0:T(2,128)(2,1)}, u32[]{:S(2)}, u32[]{:S(2)}) %all-to-all-start.4) | async-done | bytes 4194336 | tf_op jit(solution)/shard_map/all_to_all | solution.py:103
  200.5 7.3 %all-to-all-start.1 = ((bf16[32,128,128]{2,1,0:T(8,128)(2,1)}), bf16[32,128,128]{2,1,0:T(8,128)(2,1)S(1)}, u32[]{:S(2)}, u32[]{:S(2)}) async-start(bf16[32,128,128]{2,1,0:T(8,128)(2,1)} %get-tuple-element.143), calls=%async_computation.1 | async-start | bytes 2097152 | tf_op jit(solution)/shard_map/all_to_all | solution.py:142
  207.8 8.8 %reshape.516 = bf16[8192,1,256]{2,1,0:T(2,128)(2,1)} reshape(bf16[8,2,131072]{2,1,0:T(2,128)(2,1)} %all-to-all-done.4) | data formatting | bytes 8388608
  216.5 6.1 copy.71
  222.7 6.4 copy.58
  229.1 7.1 gather_fusion.10
  236.2 7.4 %all-to-all-start.3 = ((bf16[32,128,128]{2,1,0:T(8,128)(2,1)}), bf16[32,128,128]{2,1,0:T(8,128)(2,1)S(1)}, u32[]{:S(2)}, u32[]{:S(2)}) async-start(bf16[32,128,128]{2,1,0:T(8,128)(2,1)} %get-tuple-element.142), calls=%async_computation.3 | async-start | bytes 2097152 | tf_op jit(solution)/shard_map/all_to_all | solution.py:135
  243.6 7.6 %select_select_fusion.1 = bf16[32,128,1024]{2,1,0:T(8,128)(2,1)} fusion(bf16[32,128,1024]{2,1,0:T(8,128)(2,1)} %gather_fusion.10, pred[32]{0:T(512)(128)(4,1)S(1)} %compare_and_fusion.5, pred[32]{0:T(512)(128)(4,1)S(1)} %fusion.4), kind=kLoop, calls=%fused_computation.30 | loop fusion | flops 8388608 | bytes 16777280 | tf_op jit(solution)/shard_map/jit(_where)/select_n | solution.py:46
  251.2 9.8 %all-to-all-done.3 = bf16[32,128,128]{2,1,0:T(8,128)(2,1)S(1)} async-done(((bf16[32,128,128]{2,1,0:T(8,128)(2,1)}), bf16[32,128,128]{2,1,0:T(8,128)(2,1)S(1)}, u32[]{:S(2)}, u32[]{:S(2)}) %all-to-all-start.3) | async-done | bytes 1048608 | tf_op jit(solution)/shard_map/all_to_all | solution.py:135
  260.9 5.2 all-to-all-start.5
  273.2 2.1 gather_fusion.9
  275.3 4.1 broadcast_select_fusion.2
  279.4 92.4 %all-to-all-done.5 = bf16[32,128,1024]{2,1,0:T(8,128)(2,1)} async-done(((bf16[32,128,1024]{2,1,0:T(8,128)(2,1)}), bf16[32,128,1024]{2,1,0:T(8,128)(2,1)}, u32[]{:S(2)}, u32[]{:S(2)}) %all-to-all-start.5) | async-done | bytes 8388640 | tf_op jit(solution)/shard_map/all_to_all | solution.py:128
  371.8 6.2 gather_fusion.11
  378.0 4.6 broadcast_select_fusion.1
  382.6 93.0 %while.10 = (s32[]{:T(128)}, bf16[16,128,1024]{2,1,0:T(8,128)(2,1)}, bf16[16,4,128,128]{3,2,1,0:T(8,128)(2,1)}, s32[16,512]{1,0:T(8,128)S(1)}, s32[16]{0:T(128)S...) while((s32[]{:T(128)}, ...), condition=%wide.region_9.15_spmd, body=%wide.region_6.14_spmd.sunk | while | flops 272890368 | bytes 9862281 | solution.py:88
  384.1 1.0 constant_dynamic-slice_fusion.8
  389.9 1.0 constant_dynamic-slice_fusion.8
  395.7 1.0 constant_dynamic-slice_fusion.8
  401.5 1.0 constant_dynamic-slice_fusion.8
  407.3 1.0 constant_dynamic-slice_fusion.8
  413.1 1.0 constant_dynamic-slice_fusion.8
  418.9 1.0 constant_dynamic-slice_fusion.8
  424.8 1.0 constant_dynamic-slice_fusion.8
  430.6 1.0 constant_dynamic-slice_fusion.8
  436.4 1.0 constant_dynamic-slice_fusion.8
  442.2 1.0 constant_dynamic-slice_fusion.8
  448.0 1.0 constant_dynamic-slice_fusion.8
  475.6 7.1 gather_fusion.12
  482.7 7.6 %select_select_fusion = bf16[32,128,1024]{2,1,0:T(8,128)(2,1)} fusion(bf16[32,128,1024]{2,1,0:T(8,128)(2,1)} %gather_fusion.12, pred[32]{0:T(512)(128)(4,1)S(1)} %compare_and_fusion.3, pred[32]{0:T(512)(128)(4,1)S(1)} %fusion.5), kind=kLoop, calls=%fused_computation.29 | loop fusion | flops 8388608 | bytes 16777280 | tf_op jit(solution)/shard_map/jit(_where)/select_n | solution.py:46
  490.2 5.0 all-to-all-start.6
  495.2 105.8 %all-to-all-done.6 = bf16[32,128,1024]{2,1,0:T(8,128)(2,1)} async-done(((bf16[32,128,1024]{2,1,0:T(8,128)(2,1)}), bf16[32,128,1024]{2,1,0:T(8,128)(2,1)}, u32[]{:S(2)}, u32[]{:S(2)}) %all-to-all-start.6) | async-done | bytes 8388640 | tf_op jit(solution)/shard_map/all_to_all | solution.py:158
  601.1 6.2 gather_fusion.13
  607.3 2.6 broadcast_select_fusion
  609.9 98.2 %all_to_all.80 = bf16[8,256,1024]{2,1,0:T(8,128)(2,1)} all-to-all(bf16[8,256,1024]{2,1,0:T(8,128)(2,1)S(1)} %bitcast.98), channel_id=1, replica_groups=mesh['seq'=32,'head'=8] {'head'}, dimensions={0} | all-to-all | bytes 8388608 | tf_op jit(solution)/shard_map/all_to_all | solution.py:162
  708.2 6.4 copy.62
  714.6 6.3 copy.63
  (273 shorter events, 94.2 us)
Async XLA Ops:
  0.0 267.5 %copy-start = (s32[512]{0:T(512)S(1)}, s32[512]{0:T(512)}, u32[]{:S(2)}) copy-start(s32[512]{0:T(512)} %param.20) | copy-start | bytes 6148
  0.0 15.5 %copy-start.3 = (bf16[256,1024]{1,0:T(8,128)(2,1)S(1)}, bf16[256,1024]{1,0:T(8,128)(2,1)}, u32[]{:S(2)}) copy-start(bf16[256,1024]{1,0:T(8,128)(2,1)} %param.18) | copy-start | bytes 1572868
  7.9 21.2 %all-to-all-start = ((bf16[8,2,16384]{2,1,0:T(2,128)(2,1)}), bf16[8,2,16384]{2,1,0:T(2,128)(2,1)S(1)}, u32[]{:S(2)}, u32[]{:S(2)}) async-start(bf16[8,2,16384]{2,1,0:T(2,128)(2,1)} %reshape.511), calls=%async_computation | async-start | bytes 1048576 | tf_op jit(solution)/shard_map/all_to_all | solution.py:113
  29.1 75.7 %all-to-all-start.2 = ((bf16[8,2,16384]{2,1,0:T(2,128)(2,1)}), bf16[8,2,16384]{2,1,0:T(2,128)(2,1)S(1)}, u32[]{:S(2)}, u32[]{:S(2)}) async-start(bf16[8,2,16384]{2,1,0:T(2,128)(2,1)} %reshape.513), calls=%async_computation.2 | async-start | bytes 1048576 | tf_op jit(solution)/shard_map/all_to_all | solution.py:110
  104.8 7.4 %copy-start.2 = (s32[512]{0:T(512)S(1)}, s32[512]{0:T(512)}, u32[]{:S(2)}) copy-start(s32[512]{0:T(512)} %param.21) | copy-start | bytes 6148
  104.8 95.6 %all-to-all-start.4 = ((bf16[8,2,131072]{2,1,0:T(2,128)(2,1)}), bf16[8,2,131072]{2,1,0:T(2,128)(2,1)}, u32[]{:S(2)}, u32[]{:S(2)}) async-start(bf16[8,2,131072]{2,1,0:T(2,128)(2,1)} %reshape.515), calls=%async_computation.4 | async-start | bytes 8388608 | tf_op jit(solution)/shard_map/all_to_all | solution.py:103
  200.5 35.8 %all-to-all-start.1 = ((bf16[32,128,128]{2,1,0:T(8,128)(2,1)}), bf16[32,128,128]{2,1,0:T(8,128)(2,1)S(1)}, u32[]{:S(2)}, u32[]{:S(2)}) async-start(bf16[32,128,128]{2,1,0:T(8,128)(2,1)} %get-tuple-element.143), calls=%async_computation.1 | async-start | bytes 2097152 | tf_op jit(solution)/shard_map/all_to_all | solution.py:142
  236.2 24.7 %all-to-all-start.3 = ((bf16[32,128,128]{2,1,0:T(8,128)(2,1)}), bf16[32,128,128]{2,1,0:T(8,128)(2,1)S(1)}, u32[]{:S(2)}, u32[]{:S(2)}) async-start(bf16[32,128,128]{2,1,0:T(8,128)(2,1)} %get-tuple-element.142), calls=%async_computation.3 | async-start | bytes 2097152 | tf_op jit(solution)/shard_map/all_to_all | solution.py:135
  260.9 110.8 %all-to-all-start.5 = ((bf16[32,128,1024]{2,1,0:T(8,128)(2,1)}), bf16[32,128,1024]{2,1,0:T(8,128)(2,1)}, u32[]{:S(2)}, u32[]{:S(2)}) async-start(bf16[32,128,1024]{2,1,0:T(8,128)(2,1)} %select_select_fusion.1), calls=%async_computation.5 | async-start | bytes 16777216 | tf_op jit(solution)/shard_map/all_to_all | solution.py:128
  490.2 110.8 %all-to-all-start.6 = ((bf16[32,128,1024]{2,1,0:T(8,128)(2,1)}), bf16[32,128,1024]{2,1,0:T(8,128)(2,1)}, u32[]{:S(2)}, u32[]{:S(2)}) async-start(bf16[32,128,1024]{2,1,0:T(8,128)(2,1)} %select_select_fusion), calls=%async_computation.6 | async-start | bytes 16777216 | tf_op jit(solution)/shard_map/all_to_all | solution.py:158
  714.6 6.3 copy-start.1
where the time goes:
time: 729 us; the launch traced here: 721 us
  waiting for transfers between devices  298 us (41%)
  local copies, waits for them, and re-layouts  161 us (22%)
  other arithmetic  99.4 us (14%)
  blocking collectives  98.2 us (13%)
  starting transfers between devices  47.2 us (6%)
  matrix products  15.5 us (2%)
    all_to_all x1, waiting for transfers between devices, shards(): lax.all_to_all(fill_slots(mixed, slot_in, slot_count), 'seq', split_axis=...  106 us
    all_to_all x1, blocking collectives, shards(): lax.all_to_all(result.reshape(head_count, tok_dev, query_cols), 'head', s...  98.2 us
    all_to_all x1, waiting for transfers between devices, shards(): lax.all_to_all(fill_slots(query_grp, slot_out, slot_count), 'seq', split_...  92.4 us
    all_to_all x1, waiting for transfers between devices, shards(): lax.all_to_all(queries.reshape(1, tok_dev, queries.shape[1]), 'head', spl...  82.6 us
    unnamed x3, other arithmetic  51.4 us
    dynamic_slice x80, local copies, waits for them, and re-layouts, attend(): lax.map(one_block, (query_blocks, key_win, value_win, query_rank, query_d...  44.2 us
    unnamed x19, local copies, waits for them, and re-layouts  25.6 us
    reshape x1, local copies, waits for them, and re-layouts, shards(): queries.reshape(1, tok_dev, queries.shape[1])  17.8 us
  transfers between devices with their start and end apart: 7, of which 5 were waited for; matrix products, arithmetic and copies ran while one was open for 18% of the time, Pallas kernels for 0%

commit v1 on v0

v1 whole, which is shorter than its diff:
```python
import functools
import math

import jax
import jax.numpy as jnp
from jax import lax
from jax.experimental import pallas as pl
from jax.experimental.pallas import tpu as pltpu
from jax.sharding import PartitionSpec as P

HEAD_DIM = 128
BLOCK = 128
BLOCKS = 512
GROUP = 16
KV = 8
SEQ = 32
ZS = 8
ITEMS = 64
WINDOW = 3
NEED = 2 * WINDOW
CHUNKS = 4
FAST = 16
SLOW = 64
MESH = pl.DeviceIdType.MESH
SCALE = math.log2(math.e) / math.sqrt(HEAD_DIM)


def table_kernel(balance_ref, doc_ref, table_ref):
    seq = lax.axis_index("seq")
    z = lax.axis_index("head")
    f32 = jnp.float32
    balance = balance_ref[...]
    doc = doc_ref[...].astype(f32)
    rows = lax.broadcasted_iota(jnp.int32, (BLOCKS, BLOCKS), 0)
    cols = lax.broadcasted_iota(jnp.int32, (BLOCKS, BLOCKS), 1)
    doc_col = jnp.sum(jnp.where(rows == cols, doc, 0.0), axis=1, keepdims=True)
    label = jnp.sum(jnp.where(rows == balance, doc_col, 0.0), axis=0, keepdims=True)
    position = lax.broadcasted_iota(jnp.int32, (1, BLOCKS), 1)
    z_of = balance % GROUP // 2
    item = balance // GROUP * 2 + balance % 2
    zs = lax.broadcasted_iota(jnp.int32, (ZS, BLOCKS), 0)
    uses = (zs == z_of).astype(f32)
    wanted = jnp.zeros((ZS, BLOCKS), f32)
    valid = []
    for w in range(1, WINDOW + 1):
        same = (position % GROUP >= w) & (pltpu.roll(label, w, 1) == label)
        same = same.astype(f32)
        valid.append(same)
        wanted = jnp.maximum(wanted, pltpu.roll(uses * same, BLOCKS - w, 1))
    to_mine = jnp.sum(jnp.where(zs == z, wanted, 0.0), axis=0, keepdims=True)
    sends = jnp.where(z_of == z, wanted, 0.0)
    receives = uses * to_mine
    members = jnp.concatenate([sends, receives], axis=0)
    before = (rows < cols).astype(f32).astype(jnp.bfloat16)
    ranks = jnp.dot(members.astype(jnp.bfloat16), before, preferred_element_type=f32)
    counts = jnp.zeros((ZS, 1), f32)
    for other in range(ZS):
        count = jnp.sum(uses * wanted[other : other + 1, :], axis=1, keepdims=True)
        own = lax.broadcasted_iota(jnp.int32, (ZS, 1), 0) == other
        counts = jnp.maximum(counts, jnp.where(own, 0.0, count))
    most = jnp.max(counts, axis=0, keepdims=True)
    rank_in = jnp.sum(receives * ranks[ZS:, :], axis=0, keepdims=True)
    z_float = z_of.astype(f32)
    item_float = item.astype(f32)
    lanes = lax.broadcasted_iota(jnp.int32, (ITEMS, 128), 1)
    table = jnp.where(lanes == 14, most, 0.0)
    slot = lax.broadcasted_iota(jnp.int32, (ITEMS, BLOCKS), 0).astype(f32)
    for other in range(ZS):
        rank = jnp.where(members[other : other + 1, :] > 0.0, ranks[other : other + 1, :], -1.0)
        picked = jnp.sum(jnp.where(slot == rank, item_float, 0.0), axis=1, keepdims=True)
        table = jnp.where(lanes == other, picked, table)
    row64 = lax.broadcasted_iota(jnp.int32, (ITEMS, BLOCKS), 0)
    consumer = row64 // 2 * GROUP + z * 2 + row64 % 2
    match = consumer == balance
    for fast, lane in ((FAST, 8), (SLOW, 11)):
        place = jnp.where(z_of == z, item_float, ITEMS + z_float * fast + rank_in)
        for w in range(1, WINDOW + 1):
            source = pltpu.roll(place, w, 1) * valid[w - 1]
            found = jnp.sum(jnp.where(match, source, 0.0), axis=1, keepdims=True)
            table = jnp.where(lanes == lane + w - 1, found, table)
    in_use = valid[0] + valid[0] * valid[1] + valid[0] * valid[1] * valid[2]
    for t in range(2):
        mine = balance == seq * GROUP + z * 2 + t
        used = jnp.sum(jnp.where(mine, in_use, 0.0), axis=1, keepdims=True)
        table = jnp.where(lanes == 15 + t, used, table)
    table_ref[...] = table.astype(jnp.int32)


def make_table(balance, doc_block):
    return pl.pallas_call(
        table_kernel,
        out_shape=jax.ShapeDtypeStruct((ITEMS, 128), jnp.int32),
        in_specs=[pl.BlockSpec(memory_space=pltpu.VMEM)] * 2,
        out_specs=pl.BlockSpec(memory_space=pltpu.VMEM),
        name="table",
    )(balance.reshape(1, BLOCKS), doc_block.reshape(1, BLOCKS))


def exchange_kernel(cap, table_ref, key_ref, value_ref, out_ref, *scratch):
    pieces, landed, held, packed, final, sends, arrivals, local = scratch_lists(scratch)
    seq = lax.axis_index("seq")
    z = lax.axis_index("head")
    place_lane = 8 if cap == FAST else 11

    def plane_peer(step):
        step = step * 13 % SEQ
        y = (seq // 8 + step // 8) % 4
        x = (seq // 2 + step // 2) % 4
        core = (seq + step) % 2
        return y * 8 + x * 2 + core

    barrier = pltpu.get_barrier_semaphore()

    def greet_plane(step, carry):
        pl.semaphore_signal(barrier, inc=1, device_id=(plane_peer(step), z), device_id_type=MESH)
        return carry

    def greet_z(step, carry):
        pl.semaphore_signal(barrier, inc=1, device_id=(seq, (z + step) % ZS), device_id_type=MESH)
        return carry

    lax.fori_loop(1, SEQ, greet_plane, 0)
    lax.fori_loop(1, ZS, greet_z, 0)

    for chunk in range(CHUNKS):
        source = key_ref if chunk < 2 else value_ref
        for head in range(KV):
            for quarter in range(4):
                for t in range(2):
                    row = t * BLOCK + quarter * 32 + chunk % 2 * 16
                    pieces[chunk][head * 4 + quarter, t] = source[
                        row : row + 16, head * HEAD_DIM : (head + 1) * HEAD_DIM
                    ]
    pl.semaphore_wait(barrier, SEQ - 1 + ZS - 1)

    def spread(chunk):
        def send(step, carry):
            peer = plane_peer(step)
            pltpu.make_async_remote_copy(
                src_ref=pieces[chunk].at[peer],
                dst_ref=landed[chunk].at[seq],
                send_sem=sends.at[0, chunk],
                recv_sem=arrivals.at[0, chunk],
                device_id=(peer, z),
                device_id_type=MESH,
            ).start()
            return carry

        lax.fori_loop(1, SEQ, send, 0)
        landed[chunk][seq] = pieces[chunk][seq]

    def across(chunk):
        whole = landed[chunk].at[pl.ds(0, SEQ - 1)]
        pltpu.make_async_copy(whole, whole, arrivals.at[0, chunk]).wait()

        def pack(step, carry):
            other = (z + step) % ZS
            for k in range(cap):
                index = table_ref[k, other]
                packed[chunk][other, k] = landed[chunk][index // 2, index % 2]
            pltpu.make_async_remote_copy(
                src_ref=packed[chunk].at[other],
                dst_ref=held[chunk].at[pl.ds(ITEMS + z * cap, cap)],
                send_sem=sends.at[1, chunk],
                recv_sem=arrivals.at[1, chunk],
                device_id=(seq, other),
                device_id_type=MESH,
            ).start()
            return carry

        lax.fori_loop(1, ZS, pack, 0)

        def keep(k, carry):
            held[chunk][2 * k] = landed[chunk][k, 0]
            held[chunk][2 * k + 1] = landed[chunk][k, 1]
            return carry

        lax.fori_loop(0, SEQ, keep, 0)

        def blank(k, carry):
            held[chunk][ITEMS + z * cap + k] = jnp.zeros((16, HEAD_DIM), jnp.bfloat16)
            return carry

        lax.fori_loop(0, cap, blank, 0)

    def deliver(chunk):
        whole = held[chunk].at[pl.ds(0, (ZS - 1) * cap)]
        pltpu.make_async_copy(whole, whole, arrivals.at[1, chunk]).wait()

        def fill(peer):
            for n in range(NEED):
                index = table_ref[peer * 2 + n // WINDOW, place_lane + n % WINDOW]
                final[chunk][peer, n] = held[chunk][index]

        def pack(step, carry):
            peer = plane_peer(step)
            fill(peer)
            pltpu.make_async_remote_copy(
                src_ref=final[chunk].at[peer],
                dst_ref=out_ref.at[chunk, seq],
                send_sem=sends.at[2, chunk],
                recv_sem=arrivals.at[2, chunk],
                device_id=(peer, z),
                device_id_type=MESH,
            ).start()
            return carry

        lax.fori_loop(1, SEQ, pack, 0)
        fill(seq)
        pltpu.make_async_copy(final[chunk].at[seq], out_ref.at[chunk, seq], local.at[chunk]).start()

    for chunk in range(CHUNKS):
        spread(chunk)
    for chunk in range(CHUNKS):
        across(chunk)
    for chunk in range(CHUNKS):
        deliver(chunk)
    for chunk in range(CHUNKS):
        pltpu.make_async_copy(final[chunk].at[seq], out_ref.at[chunk, seq], local.at[chunk]).wait()
        whole = out_ref.at[chunk, pl.ds(0, SEQ - 1)]
        pltpu.make_async_copy(whole, whole, arrivals.at[2, chunk]).wait()
        gone = pieces[chunk].at[pl.ds(0, SEQ - 1)]
        pltpu.make_async_copy(gone, gone, sends.at[0, chunk]).wait()
        gone = packed[chunk].at[pl.ds(0, ZS - 1)]
        pltpu.make_async_copy(gone, gone, sends.at[1, chunk]).wait()
        gone = final[chunk].at[pl.ds(0, SEQ - 1)]
        pltpu.make_async_copy(gone, gone, sends.at[2, chunk]).wait()


def scratch_lists(scratch):
    lists = [scratch[k * CHUNKS : (k + 1) * CHUNKS] for k in range(5)]
    return (*lists, *scratch[5 * CHUNKS :])


def exchange(cap, ident, table, keys, values):
    tile = (16, HEAD_DIM)
    shapes = ((SEQ, 2), (SEQ, 2), (ITEMS + ZS * cap,), (ZS, cap), (SEQ, NEED))
    buffers = [pltpu.VMEM(s + tile, jnp.bfloat16) for s in shapes for _ in range(CHUNKS)]
    return pl.pallas_call(
        functools.partial(exchange_kernel, cap),
        out_shape=jax.ShapeDtypeStruct((CHUNKS, SEQ, NEED) + tile, jnp.bfloat16),
        in_specs=[
            pl.BlockSpec(memory_space=pltpu.SMEM),
            pl.BlockSpec(memory_space=pltpu.VMEM),
            pl.BlockSpec(memory_space=pltpu.VMEM),
        ],
        out_specs=pl.BlockSpec(memory_space=pl.ANY),
        scratch_shapes=buffers
        + [
            pltpu.SemaphoreType.DMA((3, CHUNKS)),
            pltpu.SemaphoreType.DMA((3, CHUNKS)),
            pltpu.SemaphoreType.DMA((CHUNKS,)),
        ],
        compiler_params=pltpu.CompilerParams(
            collective_id=ident, has_side_effects=True, vmem_limit_bytes=48 * 1024 * 1024
        ),
        name=f"exchange_{cap}",
    )(table, keys, values)


def attend_kernel(used_ref, query_ref, key_ref, value_ref, window_ref, out_ref):
    group = query_ref.shape[1] // HEAD_DIM
    ones = jnp.ones((BLOCK, HEAD_DIM), jnp.bfloat16)
    above = lax.broadcasted_iota(jnp.int32, (BLOCK, BLOCK), 1) > lax.broadcasted_iota(
        jnp.int32, (BLOCK, BLOCK), 0
    )

    def block(t, windows):
        rows = slice(t * BLOCK, (t + 1) * BLOCK)
        keys = [key_ref[rows, :]]
        values = [value_ref[rows, :]]
        for w in range(windows):
            n = t * WINDOW + w
            keys.append(window_ref[0:2, :, n].reshape(BLOCK, HEAD_DIM))
            values.append(window_ref[2:4, :, n].reshape(BLOCK, HEAD_DIM))
        keys = jnp.concatenate(keys, axis=0)
        values = jnp.concatenate(
            [jnp.concatenate([v, ones], axis=1) for v in values], axis=0
        )
        query = jnp.concatenate(
            [query_ref[rows, h * HEAD_DIM : (h + 1) * HEAD_DIM] for h in range(group)], axis=0
        )
        scores = lax.dot_general(
            query, keys, (((1,), (1,)), ((), ())), preferred_element_type=jnp.float32
        )
        own = scores[:, :BLOCK].reshape(group, BLOCK, BLOCK)
        own = jnp.where(above[None], -jnp.inf, own).reshape(group * BLOCK, BLOCK)
        scores = jnp.concatenate([own, scores[:, BLOCK:]], axis=1) if windows else own
        top = jnp.max(scores, axis=1, keepdims=True)
        weights = jnp.exp2((scores - top) * SCALE).astype(jnp.bfloat16)
        mixed = jnp.dot(weights, values, preferred_element_type=jnp.float32)
        result = (mixed[:, :HEAD_DIM] / mixed[:, HEAD_DIM:]).astype(jnp.bfloat16)
        for h in range(group):
            out_ref[rows, h * HEAD_DIM : (h + 1) * HEAD_DIM] = result[
                h * BLOCK : (h + 1) * BLOCK, :
            ]

    for t in range(2):
        for windows in range(WINDOW + 1):
            pl.when(used_ref[t] == windows)(functools.partial(block, t, windows))


def attend(used, queries, keys, values, window):
    tokens, width = queries.shape
    columns = width // KV
    spec = pltpu.PrefetchScalarGridSpec(
        num_scalar_prefetch=1,
        grid=(KV,),
        in_specs=[
            pl.BlockSpec((tokens, columns), lambda k, used: (0, k)),
            pl.BlockSpec((tokens, HEAD_DIM), lambda k, used: (0, k)),
            pl.BlockSpec((tokens, HEAD_DIM), lambda k, used: (0, k)),
            pl.BlockSpec((CHUNKS, 4, NEED, 16, HEAD_DIM), lambda k, used: (0, k, 0, 0, 0)),
        ],
        out_specs=pl.BlockSpec((tokens, columns), lambda k, used: (0, k)),
    )
    return pl.pallas_call(
        attend_kernel,
        out_shape=jax.ShapeDtypeStruct(queries.shape, queries.dtype),
        grid_spec=spec,
        compiler_params=pltpu.CompilerParams(vmem_limit_bytes=48 * 1024 * 1024),
        name="attend",
    )(used, queries, keys, values, window)


def shards(queries, keys, values, doc_block, balance):
    table = make_table(balance, doc_block)
    window = lax.cond(
        table[0, 14] <= FAST,
        functools.partial(exchange, FAST, 0),
        functools.partial(exchange, SLOW, 1),
        table,
        keys,
        values,
    )
    return attend(table[0, 15:17], queries, keys, values, window)


def solution(mesh):
    in_specs = (
        P(("seq", "head"), None),
        P(("seq", "head"), None),
        P(("seq", "head"), None),
        P(),
        P(),
    )
    out_specs = P(("seq", "head"), None)
    return jax.shard_map(shards, mesh=mesh, in_specs=in_specs, out_specs=out_specs, check_vma=False)
```

time: 729 us -> 103 us (0.14); the launches traced: 721 us -> 103 us
  waiting for transfers between devices: 298 us -> 0 us
  local copies, waits for them, and re-layouts: 161 us -> 2.84 us
  Pallas kernels: 0 us -> 99.4 us
  other arithmetic: 99.4 us -> 0 us
  blocking collectives: 98.2 us -> 0 us
  starting transfers between devices: 47.2 us -> 0 us
  matrix products: 15.5 us -> 0 us
    all_to_all x7 -> x0, waiting for transfers between devices: 298 us -> none  [the longest x1 106 us: shards(): lax.all_to_all(fill_slots(mixed, slot_in, slot_count), 'seq', split_axis=...]
    pallas_call x0 -> x3, Pallas kernels: none -> 99.4 us  [the longest x1 75.6 us: exchange(): pl.pallas_call(functools.partial(exchange_kernel, cap), out_shape=jax.Sha...]
    all_to_all x1 -> x0, blocking collectives: 98.2 us -> none  [shards(): lax.all_to_all(result.reshape(head_count, tok_dev, query_cols), 'head', s...]
    unnamed x3 -> x0, other arithmetic: 51.4 us -> none
    all_to_all x7 -> x0, starting transfers between devices: 47.2 us -> none  [the longest x1 7.66 us: shards(): lax.all_to_all(values.reshape(1, tok_dev, values.shape[1]), 'head', split...]
    dynamic_slice x80 -> x0, local copies, waits for them, and re-layouts: 44.2 us -> none  [attend(): lax.map(one_block, (query_blocks, key_win, value_win, query_rank, query_d...]
    gather x16 -> x0, local copies, waits for them, and re-layouts: 35.6 us -> none  [the longest x4 15.7 us: fill_slots(): picked = jnp.take(blocks, source, axis=0)]
    select_n x18 -> x0, other arithmetic: 28.7 us -> none  [the longest x3 16.8 us: fill_slots(): return jnp.where(filled.reshape(mask_shape), picked, jnp.zeros_like(picked))]
  transfers between devices with their start and end apart: 7 -> 0, of which waited for: 5 -> 0; matrix products, arithmetic and copies ran while one was open for 18% -> 0% of each run, Pallas kernels for 0% -> 0%
where the time goes in v1:
time: 103 us
  Pallas kernels  99.4 us (97%)
  local copies, waits for them, and re-layouts  2.84 us (3%)
    pallas_call x1, Pallas kernels, exchange(): pl.pallas_call(functools.partial(exchange_kernel, cap), out_shape=jax.Sha...  75.6 us
    pallas_call x1, Pallas kernels, attend(): pl.pallas_call(attend_kernel, out_shape=jax.ShapeDtypeStruct(queries.shap...  22.2 us
    unnamed x2, local copies, waits for them, and re-layouts  2.18 us

profile of v1, /device:TPU:96, one launch (start us, length us, event | category | flops | bytes accessed | tf_op | source)
XLA Modules:
  0.0 102.9 jit_solution(8034842050330477920)
XLA Ops:
  0.0 1.6 %table.1 = s32[64,128]{1,0:T(8,128)S(1)} custom-call(s32[1,512]{1,0:T(1,128)} %bitcast.5, s32[1,512]{1,0:T(1,128)} %bitcast.6), custom_call_target="tpu_custom_call" | custom-call | tf_op jit(solution)/shard_map/table/pallas_call | solution.py:90
  1.6 0.6 slice.9
  2.8 0.1 slice_bitcast_fusion.used_ref
  2.9 75.6 %conditional.1 = (bf16[4,32,6,16,128]{4,3,2,1,0:T(8,128)(2,1)S(1)}) conditional(s32[]{:T(128)} %bitcast.3, (s32[64,128]{1,0:T(8,128)S(1)}, bf16[256,1024]{1,0:T(8,128)(2,1)}, bf16[256,1024]{1,0:T(8,128)(2,1)}) %tuple.11, (s32[64,128]{1,0:T(8,128)S(1)}, bf16[256,1024]{1,0:T(8,128)(2,1)}, bf16[256,1024]{1,0:T(8,128)(2,1)}) %tuple.11), branch_computations={%region_0.0_spmd, %region_1.0_spmd} | conditional | bytes 8 | solution.py:328
  2.9 75.6 %exchange_16.1 = bf16[4,32,6,16,128]{4,3,2,1,0:T(8,128)(2,1)S(1)} custom-call(s32[64,128]{1,0:T(8,128)S(1)} %get-tuple-element.23.table_ref, bf16[256,1024]{1,0:T(8,128)(2,1)} %get-tuple-element.24.key_ref, bf16[256,1024]{1,0:T(8,128)(2,1)} %get-tuple-element.25.value_ref), custom_call_target="tpu_custom_call" | custom-call | tf_op jit(solution)/shard_map/cond/branch_1_fun/exchange_16/pallas_call | solution.py:239
  78.5 0.0 copy-start
  78.5 2.2 %copy-done = bf16[256,8192]{1,0:T(8,128)(2,1)S(1)} copy-done((bf16[256,8192]{1,0:T(8,128)(2,1)S(1)}, bf16[256,8192]{1,0:T(8,128)(2,1)}, u32[]{:S(2)}) %copy-start) | copy-done | bytes 4194328
  80.7 22.2 %attend.1 = bf16[256,8192]{1,0:T(8,128)(2,1)} custom-call(s32[2]{0:T(128)S(1)} %slice_bitcast_fusion.used_ref, bf16[256,8192]{1,0:T(8,128)(2,1)S(1)} %copy-done, bf16[256,1024]{1,0:T(8,128)(2,1)} %key_ref.1, bf16[256,1024]{1,0:T(8,128)(2,1)} %value_ref.1, bf16[4,32,6,16,128]{4,3,2,1,0:T(8,128)(2,1)S(1)} %get-tuple-element.26.window_ref), custom_call_target="tpu_custom_call" | custom-call | tf_op jit(solution)/shard_map/attend/pallas_call | solution.py:317
Async XLA Ops:
  78.5 2.2 %copy-start = (bf16[256,8192]{1,0:T(8,128)(2,1)S(1)}, bf16[256,8192]{1,0:T(8,128)(2,1)}, u32[]{:S(2)}) copy-start(bf16[256,8192]{1,0:T(8,128)(2,1)} %query_ref.1) | copy-start | bytes 12582916

commit v2 on v1

v2 whole, which is shorter than its diff:
```python
import functools
import math

import jax
import jax.numpy as jnp
from jax import lax
from jax.experimental import pallas as pl
from jax.experimental.pallas import tpu as pltpu
from jax.sharding import PartitionSpec as P

HEAD_DIM = 128
BLOCK = 128
BLOCKS = 512
GROUP = 16
KV = 8
SEQ = 32
ZS = 8
ITEMS = 64
WINDOW = 3
NEED = 2 * WINDOW
CHUNKS = 4
HEADS = KV // CHUNKS
TILES = BLOCK // 16
CAPS = (13, 16, 64)
MIB = 1024 * 1024
MESH = pl.DeviceIdType.MESH
SCALE = math.log2(math.e) / math.sqrt(HEAD_DIM)


def table_kernel(balance_ref, doc_ref, table_ref, branch_ref):
    seq = lax.axis_index("seq")
    z = lax.axis_index("head")
    f32 = jnp.float32
    balance = balance_ref[...]
    doc = doc_ref[...].astype(f32)
    rows = lax.broadcasted_iota(jnp.int32, (BLOCKS, BLOCKS), 0)
    cols = lax.broadcasted_iota(jnp.int32, (BLOCKS, BLOCKS), 1)
    doc_col = jnp.sum(jnp.where(rows == cols, doc, 0.0), axis=1, keepdims=True)
    label = jnp.sum(jnp.where(rows == balance, doc_col, 0.0), axis=0, keepdims=True)
    position = lax.broadcasted_iota(jnp.int32, (1, BLOCKS), 1)
    z_of = balance % GROUP // 2
    item = balance // GROUP * 2 + balance % 2
    zs = lax.broadcasted_iota(jnp.int32, (ZS, BLOCKS), 0)
    uses = (zs == z_of).astype(f32)
    wanted = jnp.zeros((ZS, BLOCKS), f32)
    valid = []
    for w in range(1, WINDOW + 1):
        same = (position % GROUP >= w) & (pltpu.roll(label, w, 1) == label)
        same = same.astype(f32)
        valid.append(same)
        wanted = jnp.maximum(wanted, pltpu.roll(uses * same, BLOCKS - w, 1))
    to_mine = jnp.sum(jnp.where(zs == z, wanted, 0.0), axis=0, keepdims=True)
    sends = jnp.where(z_of == z, wanted, 0.0)
    receives = uses * to_mine
    members = jnp.concatenate([sends, receives], axis=0)
    before = (rows < cols).astype(f32).astype(jnp.bfloat16)
    ranks = jnp.dot(members.astype(jnp.bfloat16), before, preferred_element_type=f32)
    counts = jnp.zeros((ZS, 1), f32)
    for other in range(ZS):
        count = jnp.sum(uses * wanted[other : other + 1, :], axis=1, keepdims=True)
        own = lax.broadcasted_iota(jnp.int32, (ZS, 1), 0) == other
        counts = jnp.maximum(counts, jnp.where(own, 0.0, count))
    most = jnp.max(counts)
    branch = jnp.int32(0)
    for cap in CAPS[:-1]:
        branch = branch + (most > cap).astype(jnp.int32)
    branch_ref[0] = branch
    rank_in = jnp.sum(receives * ranks[ZS:, :], axis=0, keepdims=True)
    item_float = item.astype(f32)
    lanes = lax.broadcasted_iota(jnp.int32, (ITEMS, 128), 1)
    table = jnp.zeros((ITEMS, 128), f32)
    slot = lax.broadcasted_iota(jnp.int32, (ITEMS, BLOCKS), 0)
    for other in range(ZS):
        rank = jnp.where(members[other : other + 1, :] > 0.0, ranks[other : other + 1, :], -1.0)
        picked = jnp.sum(
            jnp.where(slot.astype(f32) == rank, item_float, 0.0), axis=1, keepdims=True
        )
        table = jnp.where(lanes == other, picked, table)
    match = slot // 2 * GROUP + z * 2 + slot % 2 == balance
    place = jnp.where(z_of == z, item_float, ITEMS + rank_in)
    region = jnp.where(z_of == z, 0.0, z_of.astype(f32))
    for lane, what in ((8, place), (11, region)):
        for w in range(1, WINDOW + 1):
            source = pltpu.roll(what, w, 1) * valid[w - 1]
            found = jnp.sum(jnp.where(match, source, 0.0), axis=1, keepdims=True)
            table = jnp.where(lanes == lane + w - 1, found, table)
    in_use = valid[0] + valid[0] * valid[1] + valid[0] * valid[1] * valid[2]
    for t in range(2):
        mine = balance == seq * GROUP + z * 2 + t
        used = jnp.sum(jnp.where(mine, in_use, 0.0), axis=1, keepdims=True)
        table = jnp.where(lanes == 15 + t, used, table)
    table_ref[...] = table.astype(jnp.int32)


def make_table(balance, doc_block):
    return pl.pallas_call(
        table_kernel,
        out_shape=(
            jax.ShapeDtypeStruct((ITEMS, 128), jnp.int32),
            jax.ShapeDtypeStruct((1,), jnp.int32),
        ),
        in_specs=[pl.BlockSpec(memory_space=pltpu.VMEM)] * 2,
        out_specs=(
            pl.BlockSpec(memory_space=pltpu.VMEM),
            pl.BlockSpec(memory_space=pltpu.SMEM),
        ),
        name="table",
    )(balance.reshape(1, BLOCKS), doc_block.reshape(1, BLOCKS))


def head_columns(head, width=HEAD_DIM):
    start = head * width
    return pl.ds(start if isinstance(start, int) else pl.multiple_of(start, width), width)


def softmax_mix(query, keys, values, above):
    scores = lax.dot_general(
        query, keys, (((1,), (1,)), ((), ())), preferred_element_type=jnp.float32
    )
    own = jnp.where(above, -jnp.inf, scores[:, :BLOCK])
    if keys.shape[0] > BLOCK:
        scores = jnp.concatenate([own, scores[:, BLOCK:]], axis=1)
    else:
        scores = own
    top = jnp.max(scores, axis=1, keepdims=True)
    weights = jnp.exp2((scores - top) * SCALE).astype(jnp.bfloat16)
    mixed = jnp.dot(weights, values, preferred_element_type=jnp.float32)
    return (mixed[:, :HEAD_DIM] / mixed[:, HEAD_DIM:]).astype(jnp.bfloat16)


def causal():
    return lax.broadcasted_iota(jnp.int32, (BLOCK, BLOCK), 1) > lax.broadcasted_iota(
        jnp.int32, (BLOCK, BLOCK), 0
    )


def with_ones(values):
    return jnp.concatenate([values, jnp.ones((BLOCK, HEAD_DIM), jnp.bfloat16)], axis=1)


def exchange_kernel(cap, table_ref, key_ref, value_ref, query_ref, last_ref, part_ref, *scratch):
    pieces, landed, held, packed, final = [
        scratch[k * CHUNKS : (k + 1) * CHUNKS] for k in range(5)
    ]
    rest = scratch[5 * CHUNKS :]
    windows = rest[: CHUNKS - 1] + (last_ref,)
    query, mixed = rest[CHUNKS - 1], rest[CHUNKS : 2 * CHUNKS - 1]
    sends, arrivals, local = rest[2 * CHUNKS - 1 :]
    seq = lax.axis_index("seq")
    z = lax.axis_index("head")
    width = mixed[0].shape[1]

    def plane_peer(step):
        step = step * 13 % SEQ
        y = (seq // 8 + step // 8) % 4
        x = (seq // 2 + step // 2) % 4
        core = (seq + step) % 2
        return y * 8 + x * 2 + core

    barrier = pltpu.get_barrier_semaphore()

    def greet_plane(step, carry):
        pl.semaphore_signal(barrier, inc=1, device_id=(plane_peer(step), z), device_id_type=MESH)
        return carry

    def greet_z(step, carry):
        pl.semaphore_signal(barrier, inc=1, device_id=(seq, (z + step) % ZS), device_id_type=MESH)
        return carry

    lax.fori_loop(1, SEQ, greet_plane, 0)
    lax.fori_loop(1, ZS, greet_z, 0)
    fetch = pltpu.make_async_copy(
        query_ref.at[:, pl.ds(0, (CHUNKS - 1) * width)], query, local.at[CHUNKS]
    )
    fetch.start()

    for chunk in range(CHUNKS):
        for kind, source in enumerate((key_ref, value_ref)):
            for h in range(HEADS):
                for tile in range(TILES):
                    for t in range(2):
                        row = t * BLOCK + tile * 16
                        pieces[chunk][(kind * HEADS + h) * TILES + tile, t] = source[
                            row : row + 16, head_columns(chunk * HEADS + h)
                        ]
    pl.semaphore_wait(barrier, SEQ - 1 + ZS - 1)

    def spread(chunk):
        def send(step, carry):
            peer = plane_peer(step)
            pltpu.make_async_remote_copy(
                src_ref=pieces[chunk].at[peer],
                dst_ref=landed[chunk].at[seq],
                send_sem=sends.at[0, chunk],
                recv_sem=arrivals.at[0, chunk],
                device_id=(peer, z),
                device_id_type=MESH,
            ).start()
            return carry

        lax.fori_loop(1, SEQ, send, 0)
        landed[chunk][seq] = pieces[chunk][seq]

    def across(chunk):
        whole = landed[chunk].at[pl.ds(0, SEQ - 1)]
        pltpu.make_async_copy(whole, whole, arrivals.at[0, chunk]).wait()

        def pack(step, carry):
            other = (z + step) % ZS
            for k in range(cap):
                index = table_ref[k, other]
                packed[chunk][other, k] = landed[chunk][index // 2, index % 2]
            pltpu.make_async_remote_copy(
                src_ref=packed[chunk].at[other],
                dst_ref=held[chunk].at[pl.ds(ITEMS + z * cap, cap)],
                send_sem=sends.at[1, chunk],
                recv_sem=arrivals.at[1, chunk],
                device_id=(seq, other),
                device_id_type=MESH,
            ).start()
            return carry

        lax.fori_loop(1, ZS, pack, 0)

    def keep(chunk):
        def own(k, carry):
            held[chunk][2 * k] = landed[chunk][k, 0]
            held[chunk][2 * k + 1] = landed[chunk][k, 1]
            return carry

        lax.fori_loop(0, SEQ, own, 0)

        def blank(k, carry):
            held[chunk][ITEMS + z * cap + k] = jnp.zeros((16, HEAD_DIM), jnp.bfloat16)
            return carry

        lax.fori_loop(0, cap, blank, 0)

    def deliver(chunk):
        whole = held[chunk].at[pl.ds(0, (ZS - 1) * cap)]
        pltpu.make_async_copy(whole, whole, arrivals.at[1, chunk]).wait()

        def fill(peer):
            for n in range(NEED):
                row, w = peer * 2 + n // WINDOW, n % WINDOW
                index = table_ref[row, 8 + w] + table_ref[row, 11 + w] * cap
                final[chunk][peer, n] = held[chunk][index]

        def pack(step, carry):
            peer = plane_peer(step)
            fill(peer)
            pltpu.make_async_remote_copy(
                src_ref=final[chunk].at[peer],
                dst_ref=windows[chunk].at[seq],
                send_sem=sends.at[2, chunk],
                recv_sem=arrivals.at[2, chunk],
                device_id=(peer, z),
                device_id_type=MESH,
            ).start()
            return carry

        lax.fori_loop(1, SEQ, pack, 0)
        fill(seq)
        pltpu.make_async_copy(
            final[chunk].at[seq], windows[chunk].at[seq], local.at[chunk]
        ).start()

    def arrive(chunk):
        pltpu.make_async_copy(
            final[chunk].at[seq], windows[chunk].at[seq], local.at[chunk]
        ).wait()
        whole = windows[chunk].at[pl.ds(0, SEQ - 1)]
        pltpu.make_async_copy(whole, whole, arrivals.at[2, chunk]).wait()

    above = causal()

    def store(chunk):
        return pltpu.make_async_copy(mixed[chunk], part_ref.at[chunk], local.at[CHUNKS + 1 + chunk])

    def attend_chunk(chunk):
        def unit(u, carry):
            t, h = u % 2, u // 2
            rows = pl.ds(pl.multiple_of(t * BLOCK, BLOCK), BLOCK)
            head = chunk * HEADS + h
            used = table_ref[0, 15 + t]
            keys = [key_ref[rows, head_columns(head)]]
            values = [with_ones(value_ref[rows, head_columns(head)])]
            first = jnp.broadcast_to(keys[0][0:1, :], (BLOCK, HEAD_DIM))
            for w in range(WINDOW):
                tiles = pl.ds(h * TILES, TILES)
                key = windows[chunk][tiles, t * WINDOW + w].reshape(BLOCK, HEAD_DIM)
                tiles = pl.ds((HEADS + h) * TILES, TILES)
                value = windows[chunk][tiles, t * WINDOW + w].reshape(BLOCK, HEAD_DIM)
                value = with_ones(value)
                keys.append(jnp.where(used > w, key, first))
                values.append(jnp.where(used > w, value, jnp.zeros_like(value)))
            keys = jnp.concatenate(keys, axis=0)
            values = jnp.concatenate(values, axis=0)
            for g in range(8):
                block = query[rows, head_columns(head * 8 + g)]
                mixed[chunk][rows, head_columns(h * 8 + g)] = softmax_mix(
                    block, keys, values, above
                )
            return carry

        lax.fori_loop(0, 2 * HEADS, unit, 0)
        store(chunk).start()

    spread(0)
    across(0)
    spread(1)
    keep(0)
    across(1)
    spread(2)
    keep(1)
    deliver(0)
    across(2)
    spread(3)
    keep(2)
    deliver(1)
    across(3)
    keep(3)
    fetch.wait()
    arrive(0)
    attend_chunk(0)
    deliver(2)
    arrive(1)
    attend_chunk(1)
    deliver(3)
    arrive(2)
    attend_chunk(2)
    arrive(3)
    for chunk in range(CHUNKS):
        gone = pieces[chunk].at[pl.ds(0, SEQ - 1)]
        pltpu.make_async_copy(gone, gone, sends.at[0, chunk]).wait()
        gone = packed[chunk].at[pl.ds(0, ZS - 1)]
        pltpu.make_async_copy(gone, gone, sends.at[1, chunk]).wait()
        gone = final[chunk].at[pl.ds(0, SEQ - 1)]
        pltpu.make_async_copy(gone, gone, sends.at[2, chunk]).wait()
    for chunk in range(CHUNKS - 1):
        store(chunk).wait()


def exchange(ident, table, keys, values, queries):
    cap = CAPS[ident]
    tokens, width = queries.shape[0], queries.shape[1] // CHUNKS
    bf16 = jnp.bfloat16
    tile = (16, HEAD_DIM)
    shapes = ((SEQ, 2), (SEQ, 2), (ITEMS + ZS * cap,), (ZS, cap), (SEQ, NEED))
    buffers = [pltpu.VMEM(s + tile, bf16) for s in shapes for _ in range(CHUNKS)]
    buffers += [pltpu.VMEM((SEQ, NEED) + tile, bf16)] * (CHUNKS - 1)
    buffers += [pltpu.VMEM((tokens, (CHUNKS - 1) * width), bf16)]
    buffers += [pltpu.VMEM((tokens, width), bf16)] * (CHUNKS - 1)
    return pl.pallas_call(
        functools.partial(exchange_kernel, cap),
        out_shape=(
            jax.ShapeDtypeStruct((SEQ, NEED) + tile, bf16),
            jax.ShapeDtypeStruct((CHUNKS - 1, tokens, width), bf16),
        ),
        in_specs=[
            pl.BlockSpec(memory_space=pltpu.SMEM),
            pl.BlockSpec(memory_space=pltpu.VMEM),
            pl.BlockSpec(memory_space=pltpu.VMEM),
            pl.BlockSpec(memory_space=pl.ANY),
        ],
        out_specs=(pl.BlockSpec(memory_space=pl.ANY), pl.BlockSpec(memory_space=pl.ANY)),
        scratch_shapes=buffers
        + [
            pltpu.SemaphoreType.DMA((3, CHUNKS)),
            pltpu.SemaphoreType.DMA((3, CHUNKS)),
            pltpu.SemaphoreType.DMA((2 * CHUNKS,)),
        ],
        compiler_params=pltpu.CompilerParams(
            collective_id=ident, has_side_effects=True, vmem_limit_bytes=48 * MIB
        ),
        name=f"exchange_{cap}",
    )(table, keys, values, queries)


def finish_kernel(
    table_ref, query_ref, key_ref, value_ref, window_ref, part_ref, out_ref, mixed, sems
):
    step = pl.program_id(0)
    width = query_ref.shape[1]
    part_width = part_ref.shape[2]
    above = causal()

    def parts():
        return [
            pltpu.make_async_copy(
                part_ref.at[c], out_ref.at[:, pl.ds(c * part_width, part_width)], sems.at[HEADS + c]
            )
            for c in range(CHUNKS - 1)
        ]

    def store(h):
        return pltpu.make_async_copy(
            mixed.at[h], out_ref.at[:, head_columns((CHUNKS - 1) * HEADS + h, width)], sems.at[h]
        )

    @pl.when(step == 0)
    def _():
        for copy in parts():
            copy.start()

    def block(t, windows):
        rows = slice(t * BLOCK, (t + 1) * BLOCK)
        keys = [key_ref[rows, :]]
        values = [with_ones(value_ref[rows, :])]
        for w in range(windows):
            n = t * WINDOW + w
            tiles = pl.ds(step * TILES, TILES)
            keys.append(window_ref[tiles, n].reshape(BLOCK, HEAD_DIM))
            tiles = pl.ds((HEADS + step) * TILES, TILES)
            values.append(with_ones(window_ref[tiles, n].reshape(BLOCK, HEAD_DIM)))
        keys = jnp.concatenate(keys, axis=0)
        values = jnp.concatenate(values, axis=0)
        for g in range(8):
            mixed[step, rows, head_columns(g)] = softmax_mix(
                query_ref[rows, head_columns(g)], keys, values, above
            )

    for t in range(2):
        for windows in range(WINDOW + 1):
            pl.when(table_ref[0, 15 + t] == windows)(functools.partial(block, t, windows))
    store(step).start()

    @pl.when(step == HEADS - 1)
    def _():
        for h in range(HEADS):
            store(h).wait()
        for copy in parts():
            copy.wait()


def finish(table, queries, keys, values, window, part):
    tokens = queries.shape[0]
    columns = queries.shape[1] // KV
    first = (CHUNKS - 1) * HEADS
    return pl.pallas_call(
        finish_kernel,
        out_shape=jax.ShapeDtypeStruct(queries.shape, queries.dtype),
        grid=(HEADS,),
        in_specs=[
            pl.BlockSpec(memory_space=pltpu.SMEM),
            pl.BlockSpec((tokens, columns), lambda k: (0, first + k)),
            pl.BlockSpec((tokens, HEAD_DIM), lambda k: (0, first + k)),
            pl.BlockSpec((tokens, HEAD_DIM), lambda k: (0, first + k)),
            pl.BlockSpec(window.shape, lambda k: (0, 0, 0, 0)),
            pl.BlockSpec(memory_space=pl.ANY),
        ],
        out_specs=pl.BlockSpec(memory_space=pl.ANY),
        scratch_shapes=[
            pltpu.VMEM((HEADS, tokens, columns), queries.dtype),
            pltpu.SemaphoreType.DMA((HEADS + CHUNKS - 1,)),
        ],
        compiler_params=pltpu.CompilerParams(vmem_limit_bytes=40 * MIB),
        name="finish",
    )(table, queries, keys, values, window, part)


def shards(queries, keys, values, doc_block, balance):
    table, branch = make_table(balance, doc_block)
    window, part = lax.switch(
        branch[0],
        [functools.partial(exchange, ident) for ident in range(len(CAPS))],
        table,
        keys,
        values,
        queries,
    )
    return finish(table, queries, keys, values, window, part)


def solution(mesh):
    in_specs = (
        P(("seq", "head"), None),
        P(("seq", "head"), None),
        P(("seq", "head"), None),
        P(),
        P(),
    )
    out_specs = P(("seq", "head"), None)
    return jax.shard_map(shards, mesh=mesh, in_specs=in_specs, out_specs=out_specs, check_vma=False)
```

time: 103 us -> 89.3 us (0.87)
  the two profiles are of different devices: /device:TPU:96 before, /device:TPU:36 now
where the time goes in v2:
time: 89.3 us; the launch traced here: 89.1 us
  Pallas kernels  88 us (99%)
    pallas_call x1, Pallas kernels, exchange(): pl.pallas_call(functools.partial(exchange_kernel, cap), out_shape=(jax.Sh...  75.8 us
    pallas_call x1, Pallas kernels, finish(): pl.pallas_call(finish_kernel, out_shape=jax.ShapeDtypeStruct(queries.shap...  10.5 us
    pallas_call x1, Pallas kernels, make_table(): pl.pallas_call(table_kernel, out_shape=(jax.ShapeDtypeStruct((ITEMS, 128)...  1.8 us

profile of v2, /device:TPU:36, one launch (start us, length us, event | category | flops | bytes accessed | tf_op | source)
XLA Modules:
  0.0 89.1 jit_solution(12069968446655182021)
XLA Ops:
  0.0 1.8 %table.1 = (s32[64,128]{1,0:T(8,128)S(1)}, s32[1]{0:T(128)}) custom-call(s32[1,512]{1,0:T(1,128)} %bitcast.3, s32[1,512]{1,0:T(1,128)} %bitcast.4), custom_call_target="tpu_custom_call" | custom-call | tf_op jit(solution)/shard_map/table/pallas_call | solution.py:96
  2.5 76.0 %conditional.1 = ((bf16[32,6,16,128]{3,2,1,0:T(8,128)(2,1)}, bf16[3,256,2048]{2,1,0:T(8,128)(2,1)S(1)})) conditional(s32[]{:T(128)} %bitcast.2, (s32[64,128]{1,0:T(8,128)S(1)}, bf16[256,1024]{1,0:T(8,128)(2,1)}, bf16[256,1024]{1,0:T(8,128)(2,1)}, bf16[256,8192]{1,0:T(8,128)(2,1)}) %tuple.14, (s32[64,128]{1,0:T(8,128)S(1)}, ...), branch_computations={%region_0.0_spmd, %region_1.0_spmd, %region_2.0_spmd} | conditional | bytes 8 | solution.py:464
  2.5 75.8 %exchange_13.1 = (bf16[32,6,16,128]{3,2,1,0:T(8,128)(2,1)}, bf16[3,256,2048]{2,1,0:T(8,128)(2,1)S(1)}) custom-call(s32[64,128]{1,0:T(8,128)S(1)} %get-tuple-element.29.table_ref, bf16[256,1024]{1,0:T(8,128)(2,1)} %get-tuple-element.30.key_ref, bf16[256,1024]{1,0:T(8,128)(2,1)} %get-tuple-element.31.value_ref, bf16[256,8192]{1,0:T(8,128)(2,1)} %get-tuple-element.32.query_ref), custom_call_target="tpu_custom_call" | custom-call | tf_op jit(solution)/shard_map/cond/branch_0_fun/exchange_13/pallas_call | solution.py:354
  78.5 10.5 %finish.1 = bf16[256,8192]{1,0:T(8,128)(2,1)} custom-call(s32[64,128]{1,0:T(8,128)S(1)} %get-tuple-element.45.table_ref, bf16[256,8192]{1,0:T(8,128)(2,1)} %query_ref.1, bf16[256,1024]{1,0:T(8,128)(2,1)} %key_ref.1, bf16[256,1024]{1,0:T(8,128)(2,1)} %value_ref.1, bf16[32,6,16,128]{3,2,1,0:T(8,128)(2,1)} %get-tuple-element.47.window_ref, ...), custom_call_target="tpu_custom_call" | custom-call | tf_op jit(solution)/shard_map/finish/pallas_call | solution.py:440

commit v3 on v2

v3 whole, which is shorter than its diff:
```python
import functools
import math

import jax
import jax.numpy as jnp
from jax import lax
from jax.experimental import pallas as pl
from jax.experimental.pallas import tpu as pltpu
from jax.sharding import PartitionSpec as P

HEAD_DIM = 128
BLOCK = 128
BLOCKS = 512
GROUP = 16
KV = 8
SEQ = 32
ZS = 8
ITEMS = 64
WINDOW = 3
NEED = 2 * WINDOW
TILES = BLOCK // 16
CHIPS = SEQ // 2
CHUNK_HEADS = ((0,), (1, 2), (3, 4), (5, 6), (7,))
CHUNK_SIDE = (1, None, None, None, 0)
CHUNKS = len(CHUNK_HEADS)
LAST = CHUNKS - 1
PARTS = CHUNKS + 1
CAPS = (13, 14, 15, 17, 64)
MIB = 1024 * 1024
MESH = pl.DeviceIdType.MESH
SCALE = math.log2(math.e) / math.sqrt(HEAD_DIM)


def table_kernel(balance_ref, doc_ref, table_ref, branch_ref):
    seq = lax.axis_index("seq")
    z = lax.axis_index("head")
    f32 = jnp.float32
    balance = balance_ref[...]
    doc = doc_ref[...].astype(f32)
    rows = lax.broadcasted_iota(jnp.int32, (BLOCKS, BLOCKS), 0)
    cols = lax.broadcasted_iota(jnp.int32, (BLOCKS, BLOCKS), 1)
    doc_col = jnp.sum(jnp.where(rows == cols, doc, 0.0), axis=1, keepdims=True)
    label = jnp.sum(jnp.where(rows == balance, doc_col, 0.0), axis=0, keepdims=True)
    position = lax.broadcasted_iota(jnp.int32, (1, BLOCKS), 1)
    z_of = balance % GROUP // 2
    item = balance // GROUP * 2 + balance % 2
    zs = lax.broadcasted_iota(jnp.int32, (ZS, BLOCKS), 0)
    uses = (zs == z_of).astype(f32)
    wanted = jnp.zeros((ZS, BLOCKS), f32)
    valid = []
    for w in range(1, WINDOW + 1):
        same = (position % GROUP >= w) & (pltpu.roll(label, w, 1) == label)
        same = same.astype(f32)
        valid.append(same)
        wanted = jnp.maximum(wanted, pltpu.roll(uses * same, BLOCKS - w, 1))
    to_mine = jnp.sum(jnp.where(zs == z, wanted, 0.0), axis=0, keepdims=True)
    sends = jnp.where(z_of == z, wanted, 0.0)
    receives = uses * to_mine
    members = jnp.concatenate([sends, receives], axis=0)
    before = (rows < cols).astype(f32).astype(jnp.bfloat16)
    ranks = jnp.dot(members.astype(jnp.bfloat16), before, preferred_element_type=f32)
    counts = jnp.zeros((ZS, 1), f32)
    for other in range(ZS):
        count = jnp.sum(uses * wanted[other : other + 1, :], axis=1, keepdims=True)
        own = lax.broadcasted_iota(jnp.int32, (ZS, 1), 0) == other
        counts = jnp.maximum(counts, jnp.where(own, 0.0, count))
    most = jnp.max(counts)
    branch = jnp.int32(0)
    for cap in CAPS[:-1]:
        branch = branch + (most > cap).astype(jnp.int32)
    branch_ref[0] = branch
    rank_in = jnp.sum(receives * ranks[ZS:, :], axis=0, keepdims=True)
    item_float = item.astype(f32)
    lanes = lax.broadcasted_iota(jnp.int32, (ITEMS, 128), 1)
    table = jnp.zeros((ITEMS, 128), f32)
    slot = lax.broadcasted_iota(jnp.int32, (ITEMS, BLOCKS), 0)
    for other in range(ZS):
        rank = jnp.where(members[other : other + 1, :] > 0.0, ranks[other : other + 1, :], -1.0)
        picked = jnp.sum(
            jnp.where(slot.astype(f32) == rank, item_float, 0.0), axis=1, keepdims=True
        )
        table = jnp.where(lanes == other, picked, table)
    match = slot // 2 * GROUP + z * 2 + slot % 2 == balance
    place = jnp.where(z_of == z, item_float, ITEMS + rank_in)
    region = jnp.where(z_of == z, 0.0, z_of.astype(f32))
    for lane, what in ((8, place), (11, region)):
        for w in range(1, WINDOW + 1):
            source = pltpu.roll(what, w, 1) * valid[w - 1]
            found = jnp.sum(jnp.where(match, source, 0.0), axis=1, keepdims=True)
            table = jnp.where(lanes == lane + w - 1, found, table)
    in_use = valid[0] + valid[0] * valid[1] + valid[0] * valid[1] * valid[2]
    for t in range(2):
        mine = balance == seq * GROUP + z * 2 + t
        used = jnp.sum(jnp.where(mine, in_use, 0.0), axis=1, keepdims=True)
        table = jnp.where(lanes == 15 + t, used, table)
    table_ref[...] = table.astype(jnp.int32)


def make_table(balance, doc_block):
    return pl.pallas_call(
        table_kernel,
        out_shape=(
            jax.ShapeDtypeStruct((ITEMS, 128), jnp.int32),
            jax.ShapeDtypeStruct((1,), jnp.int32),
        ),
        in_specs=[pl.BlockSpec(memory_space=pltpu.VMEM)] * 2,
        out_specs=(
            pl.BlockSpec(memory_space=pltpu.VMEM),
            pl.BlockSpec(memory_space=pltpu.SMEM),
        ),
        name="table",
    )(balance.reshape(1, BLOCKS), doc_block.reshape(1, BLOCKS))


def head_columns(head, width=HEAD_DIM):
    start = head * width
    return pl.ds(start if isinstance(start, int) else pl.multiple_of(start, width), width)


def softmax_mix(query, keys, values, above):
    scores = lax.dot_general(
        query, keys, (((1,), (1,)), ((), ())), preferred_element_type=jnp.float32
    )
    own = jnp.where(above, -jnp.inf, scores[:, :BLOCK])
    if keys.shape[0] > BLOCK:
        scores = jnp.concatenate([own, scores[:, BLOCK:]], axis=1)
    else:
        scores = own
    top = jnp.max(scores, axis=1, keepdims=True)
    weights = jnp.exp2((scores - top) * SCALE).astype(jnp.bfloat16)
    mixed = jnp.dot(weights, values, preferred_element_type=jnp.float32)
    return (mixed[:, :HEAD_DIM] / mixed[:, HEAD_DIM:]).astype(jnp.bfloat16)


def causal():
    return lax.broadcasted_iota(jnp.int32, (BLOCK, BLOCK), 1) > lax.broadcasted_iota(
        jnp.int32, (BLOCK, BLOCK), 0
    )


def with_ones(values):
    return jnp.concatenate([values, jnp.ones((BLOCK, HEAD_DIM), jnp.bfloat16)], axis=1)


def exchange_kernel(cap, table_ref, key_ref, value_ref, query_ref, out_ref, *scratch):
    pieces, landed, held, packed = [scratch[k * CHUNKS : (k + 1) * CHUNKS] for k in range(4)]
    rest = scratch[4 * CHUNKS :]
    final, windows = rest[:PARTS], rest[PARTS : 2 * PARTS]
    query, mixed, sends, arrivals, deliveries, local = rest[2 * PARTS :]
    seq = lax.axis_index("seq")
    z = lax.axis_index("head")
    core = seq % 2
    chip = seq // 2
    width = query.shape[1] // KV

    def plane_peer(step):
        step = step * 5 % SEQ
        y = (seq // 8 + step // 8) % 4
        x = (seq // 2 + step // 2) % 4
        core = (seq + step) % 2
        return y * 8 + x * 2 + core

    def chip_peer(step):
        step = step * 5 % CHIPS
        return (chip // 4 + step // 4) % 4 * 4 + (chip + step) % 4

    barrier = pltpu.get_barrier_semaphore()

    def greet_plane(step, carry):
        pl.semaphore_signal(barrier, inc=1, device_id=(plane_peer(step), z), device_id_type=MESH)
        return carry

    def greet_z(step, carry):
        pl.semaphore_signal(barrier, inc=1, device_id=(seq, (z + step) % ZS), device_id_type=MESH)
        return carry

    lax.fori_loop(1, SEQ, greet_plane, 0)
    lax.fori_loop(1, ZS, greet_z, 0)
    fetch = pltpu.make_async_copy(query_ref, query, local.at[PARTS])
    fetch.start()

    for chunk, heads in enumerate(CHUNK_HEADS):
        for kind, source in enumerate((key_ref, value_ref)):
            for h, head in enumerate(heads):
                for tile in range(TILES):
                    for t in range(2):
                        row = t * BLOCK + tile * 16
                        pieces[chunk][(kind * len(heads) + h) * TILES + tile, t] = source[
                            row : row + 16, head_columns(head)
                        ]
    pl.semaphore_wait(barrier, SEQ - 1 + ZS - 1)

    def spread(chunk):
        side = CHUNK_SIDE[chunk]

        def send(piece, peer):
            pltpu.make_async_remote_copy(
                src_ref=pieces[chunk].at[piece],
                dst_ref=landed[chunk].at[seq],
                send_sem=sends.at[0, chunk],
                recv_sem=arrivals.at[0, chunk],
                device_id=(peer, z),
                device_id_type=MESH,
            ).start()

        def to_device(step, carry):
            peer = plane_peer(step)
            send(peer, peer)
            return carry

        def to_chip(step, carry):
            peer = chip_peer(step)
            send(peer, peer * 2 + side)
            return carry

        if side is None:
            lax.fori_loop(1, SEQ, to_device, 0)
            landed[chunk][seq] = pieces[chunk][seq]
            return
        lax.fori_loop(1, CHIPS, to_chip, 0)

        @pl.when(core == side)
        def _():
            landed[chunk][seq] = pieces[chunk][chip]

        @pl.when(core != side)
        def _():
            send(chip, chip * 2 + side)

    def across(chunk):
        whole = landed[chunk].at[pl.ds(0, SEQ - 1)]
        pltpu.make_async_copy(whole, whole, arrivals.at[0, chunk]).wait()

        def pack(step, carry):
            other = (z + step) % ZS
            for k in range(cap):
                index = table_ref[k, other]
                packed[chunk][other, k] = landed[chunk][index // 2, index % 2]
            pltpu.make_async_remote_copy(
                src_ref=packed[chunk].at[other],
                dst_ref=held[chunk].at[pl.ds(ITEMS + z * cap, cap)],
                send_sem=sends.at[1, chunk],
                recv_sem=arrivals.at[1, chunk],
                device_id=(seq, other),
                device_id_type=MESH,
            ).start()
            return carry

        lax.fori_loop(1, ZS, pack, 0)

    def keep(chunk):
        def own(k, carry):
            held[chunk][2 * k] = landed[chunk][k, 0]
            held[chunk][2 * k + 1] = landed[chunk][k, 1]
            return carry

        lax.fori_loop(0, SEQ, own, 0)

        def blank(k, carry):
            held[chunk][ITEMS + z * cap + k] = jnp.zeros((16, HEAD_DIM), jnp.bfloat16)
            return carry

        lax.fori_loop(0, cap, blank, 0)

    def part_slots(part):
        if part < LAST:
            return part, 0, NEED
        return LAST, (part - LAST) * WINDOW, WINDOW

    def collect(chunk):
        whole = held[chunk].at[pl.ds(0, (ZS - 1) * cap)]
        pltpu.make_async_copy(whole, whole, arrivals.at[1, chunk]).wait()

    def source_of(part):
        return seq if CHUNK_SIDE[part_slots(part)[0]] is None else chip

    def own_part(part):
        return pltpu.make_async_copy(
            final[part].at[seq], windows[part].at[source_of(part)], local.at[part]
        )

    def deliver(part):
        chunk, first, count = part_slots(part)

        def fill(peer):
            for k in range(count):
                n = first + k
                row, w = peer * 2 + n // WINDOW, n % WINDOW
                index = table_ref[row, 8 + w] + table_ref[row, 11 + w] * cap
                final[part][peer, k] = held[chunk][index]

        def pack(step, carry):
            peer = plane_peer(step)
            fill(peer)
            pltpu.make_async_remote_copy(
                src_ref=final[part].at[peer],
                dst_ref=windows[part].at[source_of(part)],
                send_sem=deliveries.at[0, part],
                recv_sem=deliveries.at[1, part],
                device_id=(peer, z),
                device_id_type=MESH,
            ).start()
            return carry

        lax.fori_loop(1, SEQ, pack, 0)
        fill(seq)
        own_part(part).start()

    def arrive(part):
        side = CHUNK_SIDE[part_slots(part)[0]]

        def take(count):
            whole = windows[part].at[pl.ds(0, count)]
            pltpu.make_async_copy(whole, whole, deliveries.at[1, part]).wait()

        def take_own():
            own_part(part).wait()
            take((SEQ if side is None else CHIPS) - 1)

        if side is None:
            take_own()
            return
        pl.when(core == side)(take_own)
        pl.when(core != side)(functools.partial(take, CHIPS))

    above = causal()

    def store(part):
        chunk, first, count = part_slots(part)
        rows = pl.ds(first // WINDOW * BLOCK, count // WINDOW * BLOCK)
        heads = CHUNK_HEADS[chunk]
        columns = pl.ds(heads[0] * width, len(heads) * width)
        return pltpu.make_async_copy(
            mixed.at[rows, columns],
            out_ref.at[rows, columns],
            local.at[PARTS + 1 + part],
        )

    def attend(part):
        chunk, first, count = part_slots(part)
        blocks = count // WINDOW
        heads = CHUNK_HEADS[chunk]

        def unit(u, carry):
            k, h = u % blocks, u // blocks
            t = k + first // WINDOW
            rows = pl.ds(pl.multiple_of(t * BLOCK, BLOCK), BLOCK)
            head = heads[0] + h
            used = table_ref[0, 15 + t]
            keys = [key_ref[rows, head_columns(head)]]
            values = [with_ones(value_ref[rows, head_columns(head)])]
            start = jnp.broadcast_to(keys[0][0:1, :], (BLOCK, HEAD_DIM))
            for w in range(WINDOW):
                tiles = pl.ds(h * TILES, TILES)
                key = windows[part][tiles, k * WINDOW + w].reshape(BLOCK, HEAD_DIM)
                tiles = pl.ds((len(heads) + h) * TILES, TILES)
                value = windows[part][tiles, k * WINDOW + w].reshape(BLOCK, HEAD_DIM)
                value = with_ones(value)
                keys.append(jnp.where(used > w, key, start))
                values.append(jnp.where(used > w, value, jnp.zeros_like(value)))
            keys = jnp.concatenate(keys, axis=0)
            values = jnp.concatenate(values, axis=0)
            for g in range(8):
                block = query[rows, head_columns(head * 8 + g)]
                mixed[rows, head_columns(head * 8 + g)] = softmax_mix(
                    block, keys, values, above
                )
            return carry

        lax.fori_loop(0, blocks * len(heads), unit, 0)
        store(part).start()

    def handler(what, part):
        pl.when(core == CHUNK_SIDE[min(part, LAST)])(functools.partial(what, part))

    spread(0)
    spread(1)
    handler(across, 0)
    across(1)
    spread(2)
    across(2)
    spread(3)
    handler(keep, 0)
    keep(1)
    handler(collect, 0)
    handler(deliver, 0)
    keep(2)
    across(3)
    spread(4)
    keep(3)
    collect(1)
    deliver(1)
    handler(across, 4)
    handler(keep, 4)
    fetch.wait()
    arrive(0)
    attend(0)
    collect(2)
    deliver(2)
    arrive(1)
    attend(1)
    collect(3)
    deliver(3)
    arrive(2)
    handler(collect, 4)
    handler(deliver, 4)
    handler(deliver, 5)
    attend(2)
    arrive(3)
    attend(3)
    arrive(4)
    attend(4)
    arrive(5)
    attend(5)

    def gone(ref, count, sem):
        whole = ref.at[pl.ds(0, count)]
        pltpu.make_async_copy(whole, whole, sem).wait()

    def drain(chunk):
        gone(packed[chunk], ZS - 1, sends.at[1, chunk])
        for part in range(PARTS):
            if part_slots(part)[0] == chunk:
                gone(final[part], SEQ - 1, deliveries.at[0, part])

    for chunk, side in enumerate(CHUNK_SIDE):
        if side is None:
            gone(pieces[chunk], SEQ - 1, sends.at[0, chunk])
            drain(chunk)
            continue
        for own, count in ((side, CHIPS - 1), (1 - side, CHIPS)):
            pl.when(core == own)(
                functools.partial(gone, pieces[chunk], count, sends.at[0, chunk])
            )
        handler(drain, chunk)
    for part in range(PARTS):
        store(part).wait()


def exchange(ident, table, keys, values, queries):
    cap = CAPS[ident]
    bf16 = jnp.bfloat16
    tile = (16, HEAD_DIM)

    def vmem(*shape):
        return pltpu.VMEM(shape + tile, bf16)

    buffers = [vmem(len(heads) * CHIPS, 2) for heads in CHUNK_HEADS]
    for shape in ((SEQ, 2), (ITEMS + ZS * cap,), (ZS, cap)):
        buffers += [vmem(*shape)] * CHUNKS
    buffers += [vmem(SEQ, NEED)] * LAST + [vmem(SEQ, WINDOW)] * 2
    buffers += [vmem(len(heads) * CHIPS, NEED) for heads in CHUNK_HEADS[:LAST]]
    buffers += [vmem(len(CHUNK_HEADS[LAST]) * CHIPS, WINDOW)] * 2
    buffers += [pltpu.VMEM(queries.shape, bf16)] * 2
    return pl.pallas_call(
        functools.partial(exchange_kernel, cap),
        out_shape=jax.ShapeDtypeStruct(queries.shape, queries.dtype),
        in_specs=[
            pl.BlockSpec(memory_space=pltpu.SMEM),
            pl.BlockSpec(memory_space=pltpu.VMEM),
            pl.BlockSpec(memory_space=pltpu.VMEM),
            pl.BlockSpec(memory_space=pl.ANY),
        ],
        out_specs=pl.BlockSpec(memory_space=pl.ANY),
        scratch_shapes=buffers
        + [
            pltpu.SemaphoreType.DMA((2, CHUNKS)),
            pltpu.SemaphoreType.DMA((2, CHUNKS)),
            pltpu.SemaphoreType.DMA((2, PARTS)),
            pltpu.SemaphoreType.DMA((2 * PARTS + 1,)),
        ],
        compiler_params=pltpu.CompilerParams(
            collective_id=ident, has_side_effects=True, vmem_limit_bytes=44 * MIB
        ),
        name=f"exchange_{cap}",
    )(table, keys, values, queries)


def shards(queries, keys, values, doc_block, balance):
    table, branch = make_table(balance, doc_block)
    return lax.switch(
        branch[0],
        [functools.partial(exchange, ident) for ident in range(len(CAPS))],
        table,
        keys,
        values,
        queries,
    )


def solution(mesh):
    in_specs = (
        P(("seq", "head"), None),
        P(("seq", "head"), None),
        P(("seq", "head"), None),
        P(),
        P(),
    )
    out_specs = P(("seq", "head"), None)
    return jax.shard_map(shards, mesh=mesh, in_specs=in_specs, out_specs=out_specs, check_vma=False)
```

time: 89.3 us -> 79.2 us (0.89)
  the two profiles are of different devices: /device:TPU:36 before, /device:TPU:1 now
where the time goes in v3:
time: 79.2 us; the launch traced here: 79.1 us
  Pallas kernels  75.9 us (96%)
  local copies, waits for them, and re-layouts  2.02 us (3%)
    pallas_call x1, Pallas kernels, exchange(): pl.pallas_call(functools.partial(exchange_kernel, cap), out_shape=jax.Sha...  74 us
    unnamed x1, local copies, waits for them, and re-layouts  2.02 us
    pallas_call x1, Pallas kernels, make_table(): pl.pallas_call(table_kernel, out_shape=(jax.ShapeDtypeStruct((ITEMS, 128)...  1.89 us

profile of v3, /device:TPU:1, one launch (start us, length us, event | category | flops | bytes accessed | tf_op | source)
XLA Modules:
  0.0 79.1 jit_solution(7371048773421107966)
XLA Ops:
  0.0 1.9 %table.1 = (s32[64,128]{1,0:T(8,128)S(1)}, s32[1]{0:T(128)}) custom-call(s32[1,512]{1,0:T(1,128)} %bitcast.3, s32[1,512]{1,0:T(1,128)} %bitcast.4), custom_call_target="tpu_custom_call" | custom-call | tf_op jit(solution)/shard_map/table/pallas_call | solution.py:100
  2.5 74.5 %conditional.1 = (bf16[256,8192]{1,0:T(8,128)(2,1)S(1)}) conditional(s32[]{:T(128)} %bitcast.2, (s32[64,128]{1,0:T(8,128)S(1)}, bf16[256,1024]{1,0:T(8,128)(2,1)}, bf16[256,1024]{1,0:T(8,128)(2,1)}, bf16[256,8192]{1,0:T(8,128)(2,1)}) %tuple.20, (s32[64,128]{1,0:T(8,128)S(1)}, bf16[256,1024]{1,0:T(8,128)(2,1)}, ...), branch_computations={%region_0.0_spmd, %region_1.0_spmd, %region_2.0_spmd, %region_3.0_... | conditional | bytes 8 | solution.py:481
  2.6 74.0 %exchange_13.1 = bf16[256,8192]{1,0:T(8,128)(2,1)S(1)} custom-call(s32[64,128]{1,0:T(8,128)S(1)} %get-tuple-element.44.table_ref, bf16[256,1024]{1,0:T(8,128)(2,1)} %get-tuple-element.50.key_ref, bf16[256,1024]{1,0:T(8,128)(2,1)} %get-tuple-element.52.value_ref, bf16[256,8192]{1,0:T(8,128)(2,1)} %get-tuple-element.54.query_ref), custom_call_target="tpu_custom_call" | custom-call | tf_op jit(solution)/shard_map/cond/branch_0_fun/exchange_13/pallas_call | solution.py:455
  77.1 2.0 %copy.17 = bf16[256,8192]{1,0:T(8,128)(2,1)} copy(bf16[256,8192]{1,0:T(8,128)(2,1)S(1)} %get-tuple-element.75) | data formatting | bytes 8388608
